TPU v7x, 256 devices: a whole 4x4x8 slice. The times are simulated.
256 devices in a mesh: row: 4 (over x), col: 4 (over z_lo, core), dp: 16 (over z_hi, y).
Axes of the slice: x: 4, y: 4, z: 8 (z_hi: 4, z_lo: 2; z = z_hi * 2 + z_lo), core: 2. Of those that a mesh axis runs over, the one named last changes fastest.
Arguments:
- tokens: bfloat16 [512, 5120], P(('col', 'dp'), 'row'), may hold values from -6 to 6
- w_gate_up: bfloat16 [2, 27648, 5120], P(None, ('col', 'dp'), 'row'), may hold values from -0.078125 to 0.078125
- w_down: bfloat16 [27648, 5120], P(('col', 'dp'), 'row'), may hold values from -0.0390625 to 0.0390625
- cotangent: bfloat16 [512, 5120], P(('col', 'dp'), 'row'), may hold values from -6 to 6
Outputs:
- output: bfloat16 [512, 5120], P(('col', 'dp'), 'row')
- d_tokens: bfloat16 [512, 5120], P(('col', 'dp'), 'row')
- d_gate_up: bfloat16 [2, 27648, 5120], P(None, ('col', 'dp'), 'row')
- d_down: bfloat16 [27648, 5120], P(('col', 'dp'), 'row')
All inputs are finite; a program needn't handle non-finite values.
Results may differ from a plain program's by a relative error of at most 0.005.
Values may be sent and summed in bfloat16 or wider, within the bound.
A program may use at most 64 MiB of HBM per device.

v0:
```python
import jax
import jax.numpy as jnp
from jax import lax
from jax.sharding import PartitionSpec as P


def reduce_rows(term_fn, local_rows):
    return lax.psum_scatter(
        term_fn(jnp.int32(0), lax.axis_size(("col", "dp")) * local_rows),
        ("col", "dp"),
        scatter_dimension=0,
        tiled=True,
    )


def local(tokens, w_gate_up, w_down, cotangent):
    local_rows = tokens.shape[0]
    gathered = lax.all_gather(tokens, ("col", "dp"), axis=0, tiled=True)
    gate_part = jnp.einsum("gfd,td->gft", w_gate_up, gathered, preferred_element_type=jnp.float32)
    gate_up = lax.psum(gate_part, "row")
    gate = gate_up[0]
    upper = gate_up[1]
    sig = jax.nn.sigmoid(gate)
    act = gate * sig
    hidden_part = (act * upper).astype(jnp.bfloat16)

    def out_term(start, count):
        return lax.dot_general(
            hidden_part, w_down, (((0,), (0,)), ((), ())), preferred_element_type=jnp.float32
        )

    output = reduce_rows(out_term, local_rows).astype(jnp.bfloat16)
    gathered_grad = lax.all_gather(cotangent, ("col", "dp"), axis=0, tiled=True)
    slope_part = jnp.einsum("fd,td->ft", w_down, gathered_grad, preferred_element_type=jnp.float32)
    slope = lax.psum(slope_part, "row")
    g_up = slope * act
    g_gate = slope * upper * sig * (1.0 + gate * (1.0 - sig))
    grads_part = jnp.stack([g_gate, g_up]).astype(jnp.bfloat16)
    d_down = jnp.einsum(
        "ft,td->fd", hidden_part, gathered_grad, preferred_element_type=jnp.float32
    ).astype(jnp.bfloat16)
    d_gate_up = jnp.einsum(
        "gft,td->gfd", grads_part, gathered, preferred_element_type=jnp.float32
    ).astype(jnp.bfloat16)

    def back_term(start, count):
        return jnp.einsum("gft,gfd->td", grads_part, w_gate_up, preferred_element_type=jnp.float32)

    d_tokens = reduce_rows(back_term, local_rows).astype(jnp.bfloat16)
    return (output, d_tokens, d_gate_up, d_down)


def solution(mesh):
    placed = (
        P(("col", "dp"), "row"),
        P(None, ("col", "dp"), "row"),
        P(("col", "dp"), "row"),
        P(("col", "dp"), "row"),
    )
    return jax.shard_map(
        local,
        mesh=mesh,
        in_specs=placed,
        out_specs=(
            P(("col", "dp"), "row"),
            P(("col", "dp"), "row"),
            P(None, ("col", "dp"), "row"),
            P(("col", "dp"), "row"),
        ),
        check_vma=False,
    )
```

profile of v0, /device:TPU:1, one launch (start us, length us, event | category | flops | bytes accessed | tf_op | source)
XLA Modules:
  0.0 1098.3 jit_solution(4775798943378094054)
XLA Ops:
  7.2 0.0 copy-start
  7.2 0.0 all-gather.5.cloned.1.call-start
  7.2 0.7 all-gather.5.cloned.1.call-update
  7.9 0.0 all-gather.3.cloned.1.call-start
  8.0 0.7 all-gather.3.cloned.1.call-update
  8.7 0.0 all-reduce.3.cloned.1.call-start
  8.7 185.9 %all-gather.5.cloned.1.call-done = bf16[512,1280]{1,0:T(8,128)(2,1)} async-done(((bf16[8,1280]{1,0:T(8,128)(2,1)}), bf16[512,1280]{1,0:T(8,128)(2,1)}) %all-gather.5.cloned.1.call-update) | async-done | bytes 1310736 | tf_op jit(solution)/shard_map/all_gather | solution.py:33
  194.7 3.3 fusion.9
  198.0 183.6 %all-gather.3.cloned.1.call-done = bf16[512,1280]{1,0:T(8,128)(2,1)} async-done(((bf16[8,1280]{1,0:T(8,128)(2,1)}), bf16[512,1280]{1,0:T(8,128)(2,1)}) %all-gather.3.cloned.1.call-update) | async-done | bytes 1310736 | tf_op jit(solution)/shard_map/all_gather | solution.py:18
  381.6 0.0 copy-done
  381.6 3.9 fusion.1
  385.5 0.0 all-reduce.3.cloned.1.call-update
  385.5 0.0 reduce-scatter.5.cloned.1.call-start
  385.6 77.3 %all-reduce.3.cloned.1.call-done = (f32[2,432,512]{2,1,0:T(8,128)}, f32[432,512]{1,0:T(8,128)}) async-done(((f32[2,432,512]{2,1,0:T(8,128)}, f32[432,512]{1,0:T(8,128)}), (f32[2,432,512]{2,1,0:T(8,128)}, f32[432,512]{1,0:T(8,128)})) %all-reduce.3.cloned.1.call-update) | async-done | bytes 2654224 | tf_op jit(solution)/shard_map/psum | solution.py:20
  462.8 2.3 fusion.5
  465.1 3.1 convolution_bitcast_fusion
  468.2 0.0 reduce-scatter.5.cloned.1.call-update
  468.2 0.0 reduce-scatter.3.cloned.1.call-start
  468.2 3.6 fusion.8
  471.9 0.0 reduce-scatter.3.cloned.1.call-update
  471.9 0.0 copy-start.1
  471.9 3.1 convolution_convert_fusion.1
  475.1 0.0 copy-done.1
  475.1 2.7 convolution_convert_fusion
  477.8 295.4 %reduce-scatter.5.cloned.1.call-done = f32[8,1280]{1,0:T(8,128)} async-done(((f32[512,1280]{1,0:T(8,128)}), f32[8,1280]{1,0:T(8,128)}) %reduce-scatter.5.cloned.1.call-update) | async-done | bytes 40976 | tf_op jit(solution)/shard_map/reduce_scatter | solution.py:8
  773.2 1.4 convert_element_type.18
  774.6 315.8 %reduce-scatter.3.cloned.1.call-done = f32[8,1280]{1,0:T(8,128)} async-done(((f32[512,1280]{1,0:T(8,128)}), f32[8,1280]{1,0:T(8,128)}) %reduce-scatter.3.cloned.1.call-update) | async-done | bytes 40976 | tf_op jit(solution)/shard_map/reduce_scatter | solution.py:8
  1090.3 1.4 convert_element_type.17
Async XLA Ops:
  7.2 374.5 %copy-start = (bf16[2,432,1280]{2,1,0:T(8,128)(2,1)S(1)}, bf16[2,432,1280]{2,1,0:T(8,128)(2,1)}, u32[]{:S(2)}) copy-start(bf16[2,432,1280]{2,1,0:T(8,128)(2,1)} %param.5) | copy-start | bytes 6635524
  7.2 187.5 %all-gather.5.cloned.1.call-start = ((), (), s32[]{:S(2)}) async-start(), calls=%async_computation.4 | async-start | bytes 1331200 | tf_op jit(solution)/shard_map/all_gather | solution.py:33
  7.9 373.7 %all-gather.3.cloned.1.call-start = ((), (), s32[]{:S(2)}) async-start(), calls=%async_computation.2 | async-start | bytes 1331200 | tf_op jit(solution)/shard_map/all_gather | solution.py:18
  8.7 454.2 %all-reduce.3.cloned.1.call-start = ((), (), s32[]{:S(2)}) async-start(), calls=%async_computation.6 | async-start | bytes 5308416 | tf_op jit(solution)/shard_map/psum | solution.py:20
  385.5 387.7 %reduce-scatter.5.cloned.1.call-start = ((), (), s32[]{:S(2)}) async-start(), calls=%async_computation.5 | async-start | bytes 2662400 | tf_op jit(solution)/shard_map/reduce_scatter | solution.py:8
  468.2 622.2 %reduce-scatter.3.cloned.1.call-start = ((), (), s32[]{:S(2)}) async-start(), calls=%async_computation.3 | async-start | bytes 2662400 | tf_op jit(solution)/shard_map/reduce_scatter | solution.py:8
  471.9 3.2 copy-start.1
Sparse Core Ops, SparseCore 0:
  9.8 184.7 all-gather.4
  196.5 185.1 all-gather.2
  385.6 77.1 all-reduce.2
  468.3 304.8 reduce-scatter.4
  775.7 314.5 reduce-scatter.2
where the time goes:
time: 1110 us; the launch traced here: 1100 us
  waiting for transfers between devices  1060 us (95%)
  matrix products  19.7 us (2%)
  between operations  13.8 us (1%)
    reduce_scatter x2, waiting for transfers between devices, reduce_rows(): lax.psum_scatter(term_fn(jnp.int32(0), lax.axis_size(('col', 'dp')) * loc...  611 us
    all_gather x1, waiting for transfers between devices, local(): gathered_grad = lax.all_gather(cotangent, ('col', 'dp'), axis=0, tiled=True)  186 us
    all_gather x1, waiting for transfers between devices, local(): gathered = lax.all_gather(tokens, ('col', 'dp'), axis=0, tiled=True)  184 us
    psum x1, waiting for transfers between devices, local(): gate_up = lax.psum(gate_part, 'row')  77.3 us
  transfers between devices with their start and end apart: 5, of which 5 were waited for; matrix products, arithmetic and copies ran while one was open for 1% of the time, Pallas kernels for 0%

commit v1 on v0

v1 whole, which is shorter than its diff:
```python
import jax
import jax.numpy as jnp
from jax import lax
from jax.experimental import pallas as pl
from jax.experimental.pallas import tpu as pltpu
from jax.sharding import PartitionSpec as P

NX, NY, NZ = 4, 4, 8
CHIPS = NY * NZ
CHUNKS = 4
PER = CHIPS // CHUNKS
ROWS = 16
CT = PER * ROWS
ZTABLE = sum(d << (3 * i) for i, d in enumerate((1, 7, 6, 3, 5, 4, 2, 0)))
BF = jnp.bfloat16
F32 = jnp.float32
MESH = pl.DeviceIdType.MESH


def kernel(tok_ref, cot_ref, wgu_hbm, wd_hbm, out_ref, dtok_ref, dgu_hbm, dd_hbm,
           w, wout, tc, xf, ps, pr, pf, hid, part, pex, rs, rr, acc, fx,
           w_sem, o_sem, xf_sem, ag_send, ag_recv, fw_send, fw_recv,
           xr_send, xr_recv, xa_send, xa_recv, pe_send, pe_recv,
           rs_send, rs_recv, fx_sem):
    x = lax.axis_index("row")
    col = lax.axis_index("col")
    dp = lax.axis_index("dp")
    k = col % 2
    y = dp % 4
    z = (dp // 4) * 2 + col // 2
    ff = wd_hbm.shape[0]
    fpad = w.shape[1]
    fx_rows = fpad // NX

    def chip(dy, dz):
        yy = (y + dy) % NY
        zz = (z + dz) % NZ
        return (x, (zz % 2) * 2 + k, (zz // 2) * 4 + yy)

    def offsets(s):
        dz = lax.shift_right_logical(jnp.int32(ZTABLE), 3 * (s // 4)) % 8
        return 3 - s % 4, dz

    partner = (x, col + 1 - 2 * k, dp)

    def xpeer(r):
        return ((x + r) % NX, col, dp)

    loads = [
        pltpu.make_async_copy(wgu_hbm.at[0], w.at[0, pl.ds(0, ff)], w_sem.at[0]),
        pltpu.make_async_copy(wgu_hbm.at[1], w.at[1, pl.ds(0, ff)], w_sem.at[1]),
        pltpu.make_async_copy(wd_hbm, w.at[2, pl.ds(0, ff)], w_sem.at[2]),
    ]
    for c in loads:
        c.start()

    bar = pltpu.get_barrier_semaphore()
    pl.semaphore_signal(bar, inc=1, device_id=partner, device_id_type=MESH)

    @pl.loop(0, CHIPS - 1)
    def _(s):
        dy, dz = offsets(s)
        pl.semaphore_signal(bar, inc=1, device_id=chip(dy, dz), device_id_type=MESH)

    @pl.loop(1, NX)
    def _(r):
        pl.semaphore_signal(bar, inc=1, device_id=xpeer(r), device_id_type=MESH)

    first = k == 0
    tok = tok_ref[...].astype(F32)
    cot = cot_ref[...].astype(F32)
    keep = jnp.where(first, tok, cot)
    xf[0] = jnp.where(first, cot, tok)
    if fpad > ff:
        w[:, pl.ds(ff, fpad - ff), :] = jnp.zeros((3, fpad - ff, w.shape[2]), BF)
    pl.semaphore_wait(bar, 1 + (CHIPS - 1) + (NX - 1))

    swap = pltpu.make_async_remote_copy(
        src_ref=xf.at[0], dst_ref=xf.at[1], send_sem=xf_sem.at[0], recv_sem=xf_sem.at[1],
        device_id=partner, device_id_type=MESH)
    swap.start()
    swap.wait()
    got = xf[1]
    own = jnp.concatenate([jnp.where(first, keep, got), jnp.where(first, got, keep)], axis=0)
    tc[k, CHIPS - 1] = own.astype(BF)

    @pl.loop(0, CHIPS - 1)
    def _(s):
        dy, dz = offsets(s)
        pltpu.make_async_remote_copy(
            src_ref=tc.at[k, CHIPS - 1], dst_ref=tc.at[k, s], send_sem=ag_send,
            recv_sem=ag_recv.at[s // PER], device_id=chip(-dy, -dz), device_id_type=MESH).start()

    for c in loads:
        c.wait()

    def local_wait(ref, sem):
        pltpu.make_async_copy(ref, ref, sem).wait()

    def forward(c):
        block = tc.at[k, pl.ds(c * PER, PER)]
        return pltpu.make_async_remote_copy(
            src_ref=block, dst_ref=block, send_sem=fw_send.at[c], recv_sem=fw_recv.at[c],
            device_id=partner, device_id_type=MESH)

    def exchange(c):
        return pltpu.make_async_remote_copy(
            src_ref=part.at[c, 1 - k], dst_ref=pex.at[c], send_sem=pe_send.at[c],
            recv_sem=pe_recv.at[c], device_id=partner, device_id_type=MESH)

    def gather_stage(c):
        @pl.when(c < CHUNKS - 1)
        def _():
            local_wait(tc.at[k, pl.ds(c * PER, PER)], ag_recv.at[c])

        @pl.when(c == CHUNKS - 1)
        def _():
            local_wait(tc.at[k, pl.ds(c * PER, PER - 1)], ag_recv.at[c])

        forward(c).start()

    def first_stage(c):
        other = tc.at[1 - k, pl.ds(c * PER, PER)]
        local_wait(other, fw_recv.at[c])

        @pl.loop(0, 3)
        def _(g):
            rows = tc[g // 2, pl.ds(c * PER, PER)].reshape(CT, w.shape[2])
            p = lax.dot_general(w[g], rows, (((1,), (1,)), ((), ())), preferred_element_type=F32)
            p = p.reshape(NX, fx_rows, CT)
            pf[c, g] = p
            ps[c, :, g] = p.astype(BF)

        @pl.loop(1, NX)
        def _(r):
            pltpu.make_async_remote_copy(
                src_ref=ps.at[c, (x + r) % NX], dst_ref=pr.at[c, r - 1], send_sem=xr_send.at[c],
                recv_sem=xr_recv.at[c], device_id=xpeer(r), device_id_type=MESH).start()

    def point_stage(c):
        local_wait(pr.at[c], xr_recv.at[c])

        def total(g):
            return (pf[c, g, x] + pr[c, 0, g].astype(F32)
                    + pr[c, 1, g].astype(F32) + pr[c, 2, g].astype(F32))

        gate = total(0)
        up = total(1)
        slope = total(2)
        sig = 1.0 / (1.0 + jnp.exp(-gate))
        act = gate * sig
        hid[c, x, 0] = (slope * up * sig * (1.0 + gate * (1.0 - sig))).astype(BF)
        hid[c, x, 1] = (slope * act).astype(BF)
        hid[c, x, 2] = (act * up).astype(BF)

        @pl.loop(1, NX)
        def _(r):
            pltpu.make_async_remote_copy(
                src_ref=hid.at[c, x], dst_ref=hid.at[c, x], send_sem=xa_send.at[c],
                recv_sem=xa_recv.at[c], device_id=xpeer(r), device_id_type=MESH).start()

    def second_stage(c):
        local_wait(hid.at[c, pl.ds(0, NX - 1)], xa_recv.at[c])

        def prod(g):
            return lax.dot_general(hid[c, :, g].reshape(fpad, CT), w[g], (((0,), (0,)), ((), ())),
                                   preferred_element_type=F32)

        part[c, 0] = prod(2)
        part[c, 1] = prod(0) + prod(1)
        exchange(c).start()

    def scatter_stage(c):
        exchange(c).wait_recv()
        both = part[c, k] + pex[c]
        rs[pl.ds(c * PER, PER)] = both.astype(BF).reshape(PER, ROWS, both.shape[1])

        @pl.loop(c * PER, c * PER + PER - jnp.where(c == CHUNKS - 1, 1, 0))
        def _(s):
            dy, dz = offsets(s)
            pltpu.make_async_remote_copy(
                src_ref=rs.at[s], dst_ref=rr.at[s], send_sem=rs_send,
                recv_sem=rs_recv.at[c], device_id=chip(dy, dz), device_id_type=MESH).start()

    @pl.loop(0, CHUNKS + 3)
    def _(t):
        @pl.when(t < CHUNKS)
        def _():
            gather_stage(t)

        @pl.when(t >= 3)
        def _():
            scatter_stage(t - 3)

        @pl.when(t < CHUNKS)
        def _():
            first_stage(t)

        @pl.when((t >= 1) & (t < CHUNKS + 1))
        def _():
            point_stage(t - 1)

        @pl.when((t >= 2) & (t < CHUNKS + 2))
        def _():
            second_stage(t - 2)

    @pl.loop(0, 3)
    def _(g):
        h = jnp.concatenate([hid[c, :, g].reshape(fpad, CT) for c in range(CHUNKS)], axis=1)
        rows = tc[g // 2].reshape(CHUNKS * CT, w.shape[2])
        wout[g] = jnp.dot(h, rows, preferred_element_type=F32).astype(BF)

    stores = [
        pltpu.make_async_copy(wout.at[0, pl.ds(0, ff)], dgu_hbm.at[0], o_sem.at[0]),
        pltpu.make_async_copy(wout.at[1, pl.ds(0, ff)], dgu_hbm.at[1], o_sem.at[1]),
        pltpu.make_async_copy(wout.at[2, pl.ds(0, ff)], dd_hbm, o_sem.at[2]),
    ]
    for c in stores:
        c.start()

    acc[...] = rs[CHIPS - 1].astype(F32)
    for c in range(CHUNKS):
        n = PER if c < CHUNKS - 1 else PER - 1
        local_wait(rr.at[pl.ds(c * PER, n)], rs_recv.at[c])
        acc[...] += jnp.sum(rr[c * PER:c * PER + n].astype(F32), axis=0)

    low = acc[0:8, :]
    high = acc[8:16, :]
    fx[0] = jnp.where(first, high, low)
    back = pltpu.make_async_remote_copy(
        src_ref=fx.at[0], dst_ref=fx.at[1], send_sem=fx_sem.at[0], recv_sem=fx_sem.at[1],
        device_id=partner, device_id_type=MESH)
    back.start()

    local_wait(tc.at[0, pl.ds(0, CHIPS - 1)], ag_send)
    local_wait(rs.at[pl.ds(0, CHIPS - 1)], rs_send)

    @pl.loop(0, CHUNKS)
    def _(c):
        forward(c).wait_send()
        local_wait(pr.at[c], xr_send.at[c])
        local_wait(pr.at[c], xa_send.at[c])
        exchange(c).wait_send()

    back.wait()
    out_ref[...] = jnp.where(first, low, fx[1]).astype(BF)
    dtok_ref[...] = jnp.where(first, fx[1], high).astype(BF)
    for c in stores:
        c.wait()


def local(tokens, w_gate_up, w_down, cotangent):
    rows, d = tokens.shape
    ff = w_down.shape[0]
    fpad = -(-ff // (NX * ROWS)) * NX * ROWS
    fq = fpad // NX
    vm = pl.BlockSpec(memory_space=pltpu.VMEM)
    hbm = pl.BlockSpec(memory_space=pl.ANY)
    dma = pltpu.SemaphoreType.DMA
    out, d_tok, d_gu, d_down = pl.pallas_call(
        kernel,
        out_shape=(
            jax.ShapeDtypeStruct((rows, d), BF),
            jax.ShapeDtypeStruct((rows, d), BF),
            jax.ShapeDtypeStruct((2, ff, d), BF),
            jax.ShapeDtypeStruct((ff, d), BF),
        ),
        in_specs=[vm, vm, hbm, hbm],
        out_specs=(vm, vm, hbm, hbm),
        scratch_shapes=[
            pltpu.VMEM((3, fpad, d), BF),
            pltpu.VMEM((3, fpad, d), BF),
            pltpu.VMEM((2, CHIPS, ROWS, d), BF),
            pltpu.VMEM((2, rows, d), F32),
            pltpu.VMEM((CHUNKS, NX, 3, fq, CT), BF),
            pltpu.VMEM((CHUNKS, NX - 1, 3, fq, CT), BF),
            pltpu.VMEM((CHUNKS, 3, NX, fq, CT), F32),
            pltpu.VMEM((CHUNKS, NX, 3, fq, CT), BF),
            pltpu.VMEM((CHUNKS, 2, CT, d), F32),
            pltpu.VMEM((CHUNKS, CT, d), F32),
            pltpu.VMEM((CHIPS, ROWS, d), BF),
            pltpu.VMEM((CHIPS, ROWS, d), BF),
            pltpu.VMEM((ROWS, d), F32),
            pltpu.VMEM((2, rows, d), F32),
            dma((3,)), dma((3,)), dma((2,)),
            dma, dma((CHUNKS,)), dma((CHUNKS,)), dma((CHUNKS,)),
            dma((CHUNKS,)), dma((CHUNKS,)), dma((CHUNKS,)), dma((CHUNKS,)),
            dma((CHUNKS,)), dma((CHUNKS,)),
            dma, dma((CHUNKS,)), dma((2,)),
        ],
        compiler_params=pltpu.CompilerParams(
            collective_id=0, has_side_effects=True, vmem_limit_bytes=56 * 2**20),
    )(tokens, cotangent, w_gate_up, w_down)
    return out, d_tok, d_gu, d_down


def solution(mesh):
    placed = (
        P(("col", "dp"), "row"),
        P(None, ("col", "dp"), "row"),
        P(("col", "dp"), "row"),
        P(("col", "dp"), "row"),
    )
    return jax.shard_map(
        local,
        mesh=mesh,
        in_specs=placed,
        out_specs=(
            P(("col", "dp"), "row"),
            P(("col", "dp"), "row"),
            P(None, ("col", "dp"), "row"),
            P(("col", "dp"), "row"),
        ),
        check_vma=False,
    )
```

time: 1110 us -> 98.8 us (0.09); the launches traced: 1100 us -> 98.6 us
  waiting for transfers between devices: 1060 us -> 0 us
  Pallas kernels: 0 us -> 91.1 us
  matrix products: 19.7 us -> 0 us
  between operations: 13.8 us -> 0.64 us
    reduce_scatter x2 -> x0, waiting for transfers between devices: 611 us -> none  [reduce_rows(): lax.psum_scatter(term_fn(jnp.int32(0), lax.axis_size(('col', 'dp')) * loc...]
    all_gather x2 -> x0, waiting for transfers between devices: 370 us -> none  [the longest x1 186 us: local(): gathered_grad = lax.all_gather(cotangent, ('col', 'dp'), axis=0, tiled=True)]
    pallas_call x0 -> x1, Pallas kernels: none -> 91.1 us  [local(): pl.pallas_call(kernel, out_shape=(jax.ShapeDtypeStruct((rows, d), BF), ja...]
    psum x1 -> x0, waiting for transfers between devices: 77.3 us -> none  [local(): gate_up = lax.psum(gate_part, 'row')]
    dot_general x6 -> x0, matrix products: 19.7 us -> none  [the longest x1 3.86 us: local(): jnp.einsum('gfd,td->gft', w_gate_up, gathered, preferred_element_type=jnp...]
  transfers between devices with their start and end apart: 5 -> 0, of which waited for: 5 -> 0; matrix products, arithmetic and copies ran while one was open for 1% -> 0% of each run, Pallas kernels for 0% -> 0%
where the time goes in v1:
time: 98.8 us; the launch traced here: 98.6 us
  Pallas kernels  91.1 us (92%)
  local copies, waits for them, and re-layouts  6.88 us (7%)
    pallas_call x1, Pallas kernels, local(): pl.pallas_call(kernel, out_shape=(jax.ShapeDtypeStruct((rows, d), BF), ja...  91.1 us
    unnamed x6, local copies, waits for them, and re-layouts  6.88 us

profile of v1, /device:TPU:1, one launch (start us, length us, event | category | flops | bytes accessed | tf_op | source)
XLA Modules:
  0.0 98.6 jit_solution(14720024747762646411)
XLA Ops:
  0.6 91.1 %shard_map.75 = (bf16[8,1280]{1,0:T(8,128)(2,1)}, bf16[8,1280]{1,0:T(8,128)(2,1)}, bf16[2,432,1280]{2,1,0:T(8,128)(2,1)}, bf16[432,1280]{1,0:T(8,128)(2,1)}) custom-call(bf16[8,1280]{1,0:T(8,128)(2,1)} %tok_ref.1, bf16[8,1280]{1,0:T(8,128)(2,1)} %cot_ref.1, bf16[2,432,1280]{2,1,0:T(8,128)(2,1)} %wgu_hbm.1, bf16[432,1280]{1,0:T(8,128)(2,1)} %wd_hbm.1), custom_call_target="tpu_custom_call" | custom-call | tf_op jit(solution)/shard_map/pallas_call | solution.py:260
  91.7 1.3 %copy.12 = bf16[8,1280]{1,0:T(8,128)(2,1)} copy(bf16[8,1280]{1,0:T(8,128)(2,1)} %get-tuple-element.8) | data formatting | bytes 40960
  93.0 1.3 %copy.13 = bf16[8,1280]{1,0:T(8,128)(2,1)} copy(bf16[8,1280]{1,0:T(8,128)(2,1)} %get-tuple-element.9) | data formatting | bytes 40960
  94.4 0.0 copy-start
  94.4 3.2 %copy.14 = bf16[2,432,1280]{2,1,0:T(8,128)(2,1)} copy(bf16[2,432,1280]{2,1,0:T(8,128)(2,1)} %get-tuple-element.10) | data formatting | bytes 4423680
  97.6 0.0 copy-done
  97.6 1.0 %copy.15 = bf16[432,1280]{1,0:T(8,128)(2,1)} copy(bf16[432,1280]{1,0:T(8,128)(2,1)S(1)} %copy-done) | data formatting | bytes 2211840
Async XLA Ops:
  94.4 3.2 %copy-start = (bf16[432,1280]{1,0:T(8,128)(2,1)S(1)}, bf16[432,1280]{1,0:T(8,128)(2,1)}, u32[]{:S(2)}) copy-start(bf16[432,1280]{1,0:T(8,128)(2,1)} %get-tuple-element.11) | copy-start | bytes 3317764

commit v2 on v1

v2 whole, which is shorter than its diff:
```python
import jax
import jax.numpy as jnp
from jax import lax
from jax.experimental import pallas as pl
from jax.experimental.pallas import tpu as pltpu
from jax.sharding import PartitionSpec as P

NX, NY, NZ = 4, 4, 8
CHIPS = NY * NZ
CHUNKS = 4
PER = CHIPS // CHUNKS
ROWS = 16
CT = PER * ROWS
HALF = CT // 2
Z_ORDER = (0, 1, 7, 2, 6, 3, 5, 4)
ZTABLE = sum(d << (3 * i) for i, d in enumerate(Z_ORDER))
ORDER = tuple((int(p[0]), int(p[1])) for p in (
    "00 01 10 20 02 11 21 30 03 12 22 31 40 50 13 23 32 41 60 51 33 42 61 52 43 62 53 63").split())
WORD = 10


def lookup(field, i):
    words = [sum(e[field] << (3 * j) for j, e in enumerate(ORDER[at:at + WORD]))
             for at in range(0, len(ORDER), WORD)]
    word = jnp.int32(words[0])
    for n, value in enumerate(words[1:], 1):
        word = jnp.where(i >= n * WORD, jnp.int32(value), word)
    return lax.shift_right_logical(word, 3 * (i % WORD)) % 8


BF = jnp.bfloat16
F32 = jnp.float32
MESH = pl.DeviceIdType.MESH


def kernel(tok_ref, cot_ref, wgu_hbm, wd_hbm, out_ref, dtok_ref, dgu_hbm, dd_hbm,
           w, wout, tc, rows, ps, pr, pf, hid, part, pex, rs, yk, yr, zs, zr, acc,
           w_sem, o_sem, az_send, az_recv, ay_send, ay_recv, fw_send, fw_recv,
           xr_send, xr_recv, xa_send, xa_recv, pe_send, pe_recv,
           sy_send, sy_recv, sz_send, sz_recv):
    x = lax.axis_index("row")
    col = lax.axis_index("col")
    dp = lax.axis_index("dp")
    k = col % 2
    y = dp % 4
    z = (dp // 4) * 2 + col // 2
    ff = wd_hbm.shape[0]
    fpad = w.shape[1]
    fx_rows = fpad // NX

    def chip(dy, dz):
        yy = (y + dy) % NY
        zz = (z + dz) % NZ
        return (x, (zz % 2) * 2 + k, (zz // 2) * 4 + yy)

    def zoff(p):
        return lax.shift_right_logical(jnp.int32(ZTABLE), 3 * p) % 8

    partner = (x, col + 1 - 2 * k, dp)

    def xpeer(r):
        return ((x + r) % NX, col, dp)

    loads = [
        pltpu.make_async_copy(wgu_hbm.at[0], w.at[0, pl.ds(0, ff)], w_sem.at[0]),
        pltpu.make_async_copy(wgu_hbm.at[1], w.at[1, pl.ds(0, ff)], w_sem.at[1]),
        pltpu.make_async_copy(wd_hbm, w.at[2, pl.ds(0, ff)], w_sem.at[2]),
    ]
    for c in loads:
        c.start()

    bar = pltpu.get_barrier_semaphore()
    pl.semaphore_signal(bar, inc=1, device_id=partner, device_id_type=MESH)

    @pl.loop(1, NZ)
    def _(d):
        pl.semaphore_signal(bar, inc=1, device_id=chip(0, d), device_id_type=MESH)

    @pl.loop(1, NY)
    def _(d):
        pl.semaphore_signal(bar, inc=1, device_id=chip(d, 0), device_id_type=MESH)

    @pl.loop(1, NX)
    def _(r):
        pl.semaphore_signal(bar, inc=1, device_id=xpeer(r), device_id_type=MESH)

    tc[0, k, 0] = jnp.concatenate(
        [tok_ref[...].astype(F32), cot_ref[...].astype(F32)], axis=0).astype(BF)
    if fpad > ff:
        w[:, pl.ds(ff, fpad - ff), :] = jnp.zeros((3, fpad - ff, w.shape[2]), BF)
    pl.semaphore_wait(bar, 1 + (NZ - 1) + (NY - 1) + (NX - 1))

    @pl.loop(1, NZ)
    def _(p):
        pltpu.make_async_remote_copy(
            src_ref=tc.at[0, k, 0], dst_ref=tc.at[p // 2, k, p % 2], send_sem=az_send,
            recv_sem=az_recv.at[p // 2], device_id=chip(0, -zoff(p)), device_id_type=MESH).start()

    for c in loads:
        c.wait()

    def local_wait(ref, sem):
        pltpu.make_async_copy(ref, ref, sem).wait()

    def forward(c):
        block = tc.at[c, k]
        return pltpu.make_async_remote_copy(
            src_ref=block, dst_ref=block, send_sem=fw_send.at[c], recv_sem=fw_recv.at[c],
            device_id=partner, device_id_type=MESH)

    def exchange(c):
        return pltpu.make_async_remote_copy(
            src_ref=part.at[c, :, pl.ds(pl.multiple_of((1 - k) * HALF, HALF), HALF)], dst_ref=pex.at[c], send_sem=pe_send.at[c],
            recv_sem=pe_recv.at[c], device_id=partner, device_id_type=MESH)

    def spread_stage(c):
        @pl.when(c == 0)
        def _():
            local_wait(tc.at[0, k, 0], az_recv.at[c])

        @pl.when(c > 0)
        def _():
            local_wait(tc.at[0, k, pl.ds(0, 2)], az_recv.at[c])

        @pl.loop(1, NY)
        def _(d):
            pltpu.make_async_remote_copy(
                src_ref=tc.at[c, k, pl.ds(0, 2)], dst_ref=tc.at[c, k, pl.ds(2 * d, 2)],
                send_sem=ay_send.at[c], recv_sem=ay_recv.at[c], device_id=chip(-d, 0),
                device_id_type=MESH).start()

    def gather_stage(c):
        local_wait(tc.at[c, k, pl.ds(2, PER - 2)], ay_recv.at[c])
        forward(c).start()

    def first_stage(c):
        local_wait(tc.at[c, 1 - k], fw_recv.at[c])

        @pl.loop(0, PER)
        def _(i):
            two = tc[c, i // (PER // 2), pl.ds((i % (PER // 2)) * 2, 2)].astype(F32)
            at = pl.ds(pl.multiple_of(c * CT + i * ROWS, ROWS), ROWS)
            rows[0, at] = two[:, 0:8].reshape(ROWS, w.shape[2]).astype(BF)
            rows[1, at] = two[:, 8:16].reshape(ROWS, w.shape[2]).astype(BF)

        @pl.loop(0, 3)
        def _(g):
            right = rows[g // 2, pl.ds(pl.multiple_of(c * CT, CT), CT)]
            p = lax.dot_general(w[g], right, (((1,), (1,)), ((), ())), preferred_element_type=F32)
            p = p.reshape(NX, fx_rows, CT)
            pf[c, g] = p
            ps[c, :, g] = p.astype(BF)

        @pl.loop(1, NX)
        def _(r):
            pltpu.make_async_remote_copy(
                src_ref=ps.at[c, (x + r) % NX], dst_ref=pr.at[c, r - 1], send_sem=xr_send.at[c],
                recv_sem=xr_recv.at[c], device_id=xpeer(r), device_id_type=MESH).start()

    def point_stage(c):
        local_wait(pr.at[c], xr_recv.at[c])

        def total(g):
            return (pf[c, g, x] + pr[c, 0, g].astype(F32)
                    + pr[c, 1, g].astype(F32) + pr[c, 2, g].astype(F32))

        gate = total(0)
        up = total(1)
        slope = total(2)
        sig = 1.0 / (1.0 + jnp.exp(-gate))
        act = gate * sig
        hid[c, x, 0] = (slope * up * sig * (1.0 + gate * (1.0 - sig))).astype(BF)
        hid[c, x, 1] = (slope * act).astype(BF)
        hid[c, x, 2] = (act * up).astype(BF)

        @pl.loop(1, NX)
        def _(r):
            pltpu.make_async_remote_copy(
                src_ref=hid.at[c, x], dst_ref=hid.at[c, x], send_sem=xa_send.at[c],
                recv_sem=xa_recv.at[c], device_id=xpeer(r), device_id_type=MESH).start()

    def second_stage(c):
        local_wait(hid.at[c, pl.ds(0, NX - 1)], xa_recv.at[c])

        def prod(g):
            return lax.dot_general(hid[c, :, g].reshape(fpad, CT), w[g], (((0,), (0,)), ((), ())),
                                   preferred_element_type=F32)

        part[c, 0] = prod(2)
        part[c, 1] = prod(0) + prod(1)
        exchange(c).start()

    def scatter_stage(c):
        exchange(c).wait_recv()

        @pl.loop(0, PER)
        def _(i):
            mine = pl.ds(pl.multiple_of(k * HALF + i * 8, 8), 8)
            theirs = pl.ds(pl.multiple_of(i * 8, 8), 8)
            both = part[c, :, mine] + pex[c, :, theirs]
            both = both.reshape(ROWS, both.shape[2])
            rs[c * PER + i] = both.astype(BF)

            @pl.when(i < 2)
            def _():
                yk[c, i] = both

        @pl.loop(1, NY)
        def _(d):
            pltpu.make_async_remote_copy(
                src_ref=rs.at[pl.ds(c * PER + 2 * d, 2)], dst_ref=yr.at[c, d - 1],
                send_sem=sy_send.at[c], recv_sem=sy_recv.at[c], device_id=chip(d, 0),
                device_id_type=MESH).start()

    def settle_stage(c):
        local_wait(yr.at[c], sy_recv.at[c])
        two = yk[c] + jnp.sum(yr[c].astype(F32), axis=0)
        zs[pl.ds(2 * c, 2)] = two.astype(BF)

        @pl.when(c == 0)
        def _():
            acc[...] = two[0]

        @pl.loop(2 * c + jnp.where(c == 0, 1, 0), 2 * c + 2)
        def _(p):
            pltpu.make_async_remote_copy(
                src_ref=zs.at[p], dst_ref=zr.at[p], send_sem=sz_send, recv_sem=sz_recv.at[c],
                device_id=chip(0, zoff(p)), device_id_type=MESH).start()

    stages = (spread_stage, gather_stage, first_stage, point_stage, second_stage,
              scatter_stage, settle_stage)

    @pl.loop(0, len(ORDER))
    def _(i):
        stage = lookup(0, i)
        c = lookup(1, i)
        for n, run in enumerate(stages):
            pl.when(stage == n)(lambda run=run: run(c))

    @pl.loop(0, 3)
    def _(g):
        h = jnp.concatenate([hid[c, :, g].reshape(fpad, CT) for c in range(CHUNKS)], axis=1)
        wout[g] = jnp.dot(h, rows[g // 2], preferred_element_type=F32).astype(BF)

    stores = [
        pltpu.make_async_copy(wout.at[0, pl.ds(0, ff)], dgu_hbm.at[0], o_sem.at[0]),
        pltpu.make_async_copy(wout.at[1, pl.ds(0, ff)], dgu_hbm.at[1], o_sem.at[1]),
        pltpu.make_async_copy(wout.at[2, pl.ds(0, ff)], dd_hbm, o_sem.at[2]),
    ]
    for c in stores:
        c.start()

    local_wait(zr.at[1], sz_recv.at[0])
    acc[...] += zr[1].astype(F32)
    for c in range(1, CHUNKS):
        local_wait(zr.at[pl.ds(2 * c, 2)], sz_recv.at[c])
        acc[...] += zr[2 * c].astype(F32) + zr[2 * c + 1].astype(F32)

    out_ref[...] = acc[0:8].astype(BF)
    dtok_ref[...] = acc[8:16].astype(BF)

    local_wait(zr.at[pl.ds(0, NZ - 1)], az_send)
    local_wait(zr.at[pl.ds(0, NZ - 1)], sz_send)

    @pl.loop(0, CHUNKS)
    def _(c):
        local_wait(yr.at[c], ay_send.at[c])
        local_wait(yr.at[c], sy_send.at[c])
        forward(c).wait_send()
        local_wait(pr.at[c], xr_send.at[c])
        local_wait(pr.at[c], xa_send.at[c])
        exchange(c).wait_send()

    for c in stores:
        c.wait()


def deliver(*refs):
    n = (len(refs) - 2) // 3
    srcs, dsts, bufs = refs[:n], refs[n:2 * n], refs[2 * n:3 * n]
    in_sems, out_sems = refs[3 * n:]
    steps = []
    for a, b, v in zip(srcs, dsts, bufs):
        rows = a.shape[-2]
        cuts = [pl.ds(0, rows)] if rows < 432 else [pl.ds(0, 224), pl.ds(224, rows - 224)]
        for g in range(a.shape[0]) if len(a.shape) == 3 else (None,):
            for cut in cuts:
                at = (cut,) if g is None else (g, cut)
                i = len(steps)
                steps.append((pltpu.make_async_copy(a.at[at], v.at[at], in_sems.at[i]),
                              pltpu.make_async_copy(v.at[at], b.at[at], out_sems.at[i])))
    for load, _ in steps:
        load.start()
    for load, store in steps:
        load.wait()
        store.start()
    for _, store in steps:
        store.wait()


def local(tokens, w_gate_up, w_down, cotangent):
    rows, d = tokens.shape
    ff = w_down.shape[0]
    fpad = -(-ff // (NX * ROWS)) * NX * ROWS
    fq = fpad // NX
    vm = pl.BlockSpec(memory_space=pltpu.VMEM)
    hbm = pl.BlockSpec(memory_space=pl.ANY)
    dma = pltpu.SemaphoreType.DMA
    results = pl.pallas_call(
        kernel,
        out_shape=(
            jax.ShapeDtypeStruct((rows, d), BF),
            jax.ShapeDtypeStruct((rows, d), BF),
            jax.ShapeDtypeStruct((2, ff, d), BF),
            jax.ShapeDtypeStruct((ff, d), BF),
        ),
        in_specs=[vm, vm, hbm, hbm],
        out_specs=(vm, vm, hbm, hbm),
        scratch_shapes=[
            pltpu.VMEM((3, fpad, d), BF),
            pltpu.VMEM((3, fpad, d), BF),
            pltpu.VMEM((CHUNKS, 2, PER, ROWS, d), BF),
            pltpu.VMEM((2, CHUNKS * CT, d), BF),
            pltpu.VMEM((CHUNKS, NX, 3, fq, CT), BF),
            pltpu.VMEM((CHUNKS, NX - 1, 3, fq, CT), BF),
            pltpu.VMEM((CHUNKS, 3, NX, fq, CT), F32),
            pltpu.VMEM((CHUNKS, NX, 3, fq, CT), BF),
            pltpu.VMEM((CHUNKS, 2, CT, d), F32),
            pltpu.VMEM((CHUNKS, 2, HALF, d), F32),
            pltpu.VMEM((CHIPS, ROWS, d), BF),
            pltpu.VMEM((CHUNKS, 2, ROWS, d), F32),
            pltpu.VMEM((CHUNKS, NY - 1, 2, ROWS, d), BF),
            pltpu.VMEM((NZ, ROWS, d), BF),
            pltpu.VMEM((NZ, ROWS, d), BF),
            pltpu.VMEM((ROWS, d), F32),
            dma((3,)), dma((3,)),
            dma, dma((CHUNKS,)), dma((CHUNKS,)), dma((CHUNKS,)), dma((CHUNKS,)), dma((CHUNKS,)),
            dma((CHUNKS,)), dma((CHUNKS,)), dma((CHUNKS,)), dma((CHUNKS,)),
            dma((CHUNKS,)), dma((CHUNKS,)),
            dma((CHUNKS,)), dma((CHUNKS,)), dma, dma((CHUNKS,)),
        ],
        compiler_params=pltpu.CompilerParams(
            collective_id=0, has_side_effects=True, vmem_limit_bytes=56 * 2**20),
    )(tokens, cotangent, w_gate_up, w_down)
    return pl.pallas_call(
        deliver,
        out_shape=tuple(jax.ShapeDtypeStruct(r.shape, r.dtype) for r in results),
        in_specs=[hbm] * len(results),
        out_specs=(hbm,) * len(results),
        scratch_shapes=[pltpu.VMEM(r.shape, r.dtype) for r in results] + [dma((8,)), dma((8,))],
        compiler_params=pltpu.CompilerParams(vmem_limit_bytes=56 * 2**20),
    )(*results)


def solution(mesh):
    placed = (
        P(("col", "dp"), "row"),
        P(None, ("col", "dp"), "row"),
        P(("col", "dp"), "row"),
        P(("col", "dp"), "row"),
    )
    return jax.shard_map(
        local,
        mesh=mesh,
        in_specs=placed,
        out_specs=(
            P(("col", "dp"), "row"),
            P(("col", "dp"), "row"),
            P(None, ("col", "dp"), "row"),
            P(("col", "dp"), "row"),
        ),
        check_vma=False,
    )
```

time: 98.8 us -> 77.8 us (0.79)
  Pallas kernels: 91.1 us -> 76.2 us
  local copies, waits for them, and re-layouts: 6.88 us -> 0 us
    pallas_call x1, Pallas kernels: 91.1 us -> 73.2 us  [local(): pl.pallas_call(kernel, out_shape=(jax.ShapeDtypeStruct((rows, d), BF), ja...]
    unnamed x6 -> x0, local copies, waits for them, and re-layouts: 6.88 us -> none
    pallas_call x0 -> x1, Pallas kernels: none -> 2.95 us  [local(): pl.pallas_call(deliver, out_shape=tuple((jax.ShapeDtypeStruct(r.shape, r....]
where the time goes in v2:
time: 77.8 us; the launch traced here: 76.8 us
  Pallas kernels  76.2 us (98%)
    pallas_call x1, Pallas kernels, local(): pl.pallas_call(kernel, out_shape=(jax.ShapeDtypeStruct((rows, d), BF), ja...  73.2 us
    pallas_call x1, Pallas kernels, local(): pl.pallas_call(deliver, out_shape=tuple((jax.ShapeDtypeStruct(r.shape, r....  2.95 us

profile of v2, /device:TPU:1, one launch (start us, length us, event | category | flops | bytes accessed | tf_op | source)
XLA Modules:
  0.0 76.8 jit_solution(7726863520079461082)
XLA Ops:
  0.6 73.2 %shard_map.75 = (bf16[8,1280]{1,0:T(8,128)(2,1)}, bf16[8,1280]{1,0:T(8,128)(2,1)}, bf16[2,432,1280]{2,1,0:T(8,128)(2,1)}, bf16[432,1280]{1,0:T(8,128)(2,1)}) custom-call(bf16[8,1280]{1,0:T(8,128)(2,1)} %tok_ref.1, bf16[8,1280]{1,0:T(8,128)(2,1)} %cot_ref.1, bf16[2,432,1280]{2,1,0:T(8,128)(2,1)} %wgu_hbm.1, bf16[432,1280]{1,0:T(8,128)(2,1)} %wd_hbm.1), custom_call_target="tpu_custom_call" | custom-call | tf_op jit(solution)/shard_map/pallas_call | solution.py:309
  73.9 2.9 %shard_map.76 = (bf16[8,1280]{1,0:T(8,128)(2,1)}, bf16[8,1280]{1,0:T(8,128)(2,1)}, bf16[2,432,1280]{2,1,0:T(8,128)(2,1)}, bf16[432,1280]{1,0:T(8,128)(2,1)}) custom-call(bf16[8,1280]{1,0:T(8,128)(2,1)} %get-tuple-element.8.refs_0_, bf16[8,1280]{1,0:T(8,128)(2,1)} %get-tuple-element.9.refs_1_, bf16[2,432,1280]{2,1,0:T(8,128)(2,1)} %get-tuple-element.10.refs_2_, ...), custom_call_target="tpu_custom_call" | custom-call | tf_op jit(solution)/shard_map/pallas_call | solution.py:345

commit v3 on v2

--- a/solution.py
+++ b/solution.py
@@ -12,15 +12,17 @@
 ROWS = 16
 CT = PER * ROWS
 HALF = CT // 2
-Z_ORDER = (0, 1, 7, 2, 6, 3, 5, 4)
+Z_ORDER = (7, 2, 6, 3, 5, 4, 0, 1)
+LAST = CHUNKS - 1
 ZTABLE = sum(d << (3 * i) for i, d in enumerate(Z_ORDER))
-ORDER = tuple((int(p[0]), int(p[1])) for p in (
-    "00 01 10 20 02 11 21 30 03 12 22 31 40 50 13 23 32 41 60 51 33 42 61 52 43 62 53 63").split())
+ORDER = (0, 1, 10, 20, 2, 11, 21, 30, 3, 12, 22, 31, 40, 50, 13, 23, 32, 41, 60, 51, 33, 42, 61,
+         52, 43, 53, 62, 70, 71, 72)
+EARLY, LATE = 4, 0
 WORD = 10
 
 
 def lookup(field, i):
-    words = [sum(e[field] << (3 * j) for j, e in enumerate(ORDER[at:at + WORD]))
+    words = [sum((e // 10, e % 10)[field] << (3 * j) for j, e in enumerate(ORDER[at:at + WORD]))
              for at in range(0, len(ORDER), WORD)]
     word = jnp.int32(words[0])
     for n, value in enumerate(words[1:], 1):
@@ -34,7 +36,7 @@
 
 
 def kernel(tok_ref, cot_ref, wgu_hbm, wd_hbm, out_ref, dtok_ref, dgu_hbm, dd_hbm,
-           w, wout, tc, rows, ps, pr, pf, hid, part, pex, rs, yk, yr, zs, zr, acc,
+           w, wout, tc, rows, ps, pr, pf, hid, part, pex, rs, yk, yr, zs, zr, lr, acc,
            w_sem, o_sem, az_send, az_recv, ay_send, ay_recv, fw_send, fw_recv,
            xr_send, xr_recv, xa_send, xa_recv, pe_send, pe_recv,
            sy_send, sy_recv, sz_send, sz_recv):
@@ -53,6 +55,9 @@
         zz = (z + dz) % NZ
         return (x, (zz % 2) * 2 + k, (zz // 2) * 4 + yy)
 
+    def near(i):
+        return jnp.where(i == 2, 2, 2 * i + 1)
+
     def zoff(p):
         return lax.shift_right_logical(jnp.int32(ZTABLE), 3 * p) % 8
 
@@ -76,25 +81,32 @@
     def _(d):
         pl.semaphore_signal(bar, inc=1, device_id=chip(0, d), device_id_type=MESH)
 
-    @pl.loop(1, NY)
-    def _(d):
-        pl.semaphore_signal(bar, inc=1, device_id=chip(d, 0), device_id_type=MESH)
+    @pl.loop(0, (NY - 1) * 3)
+    def _(i):
+        pl.semaphore_signal(bar, inc=1, device_id=chip(1 + i // 3, i % 3 - 1), device_id_type=MESH)
 
     @pl.loop(1, NX)
     def _(r):
         pl.semaphore_signal(bar, inc=1, device_id=xpeer(r), device_id_type=MESH)
 
-    tc[0, k, 0] = jnp.concatenate(
+    tc[LAST, k, 0] = jnp.concatenate(
         [tok_ref[...].astype(F32), cot_ref[...].astype(F32)], axis=0).astype(BF)
     if fpad > ff:
         w[:, pl.ds(ff, fpad - ff), :] = jnp.zeros((3, fpad - ff, w.shape[2]), BF)
-    pl.semaphore_wait(bar, 1 + (NZ - 1) + (NY - 1) + (NX - 1))
-
-    @pl.loop(1, NZ)
-    def _(p):
-        pltpu.make_async_remote_copy(
-            src_ref=tc.at[0, k, 0], dst_ref=tc.at[p // 2, k, p % 2], send_sem=az_send,
-            recv_sem=az_recv.at[p // 2], device_id=chip(0, -zoff(p)), device_id_type=MESH).start()
+    pl.semaphore_wait(bar, 1 + (NZ - 1) + (NY - 1) * 3 + (NX - 1))
+
+    mine = tc.at[LAST, k, 0]
+
+    def along_z(start, stop):
+        @pl.loop(start, stop)
+        def _(i):
+            p = i + jnp.where(i >= 2 * LAST, 1, 0)
+            pltpu.make_async_remote_copy(
+                src_ref=mine, dst_ref=tc.at[p // 2, k, p % 2], send_sem=az_send,
+                recv_sem=az_recv.at[p // 2], device_id=chip(0, -zoff(p)),
+                device_id_type=MESH).start()
+
+    along_z(0, EARLY)
 
     for c in loads:
         c.wait()
@@ -114,23 +126,29 @@
             recv_sem=pe_recv.at[c], device_id=partner, device_id_type=MESH)
 
     def spread_stage(c):
-        @pl.when(c == 0)
-        def _():
-            local_wait(tc.at[0, k, 0], az_recv.at[c])
-
-        @pl.when(c > 0)
-        def _():
-            local_wait(tc.at[0, k, pl.ds(0, 2)], az_recv.at[c])
-
-        @pl.loop(1, NY)
-        def _(d):
+        @pl.when(c == LAST)
+        def _():
+            local_wait(tc.at[c, k, 1], az_recv.at[c])
+
+        @pl.when(c < LAST)
+        def _():
+            local_wait(tc.at[c, k, pl.ds(0, 2)], az_recv.at[c])
+
+        @pl.loop(0, NY - 1)
+        def _(i):
+            d = near(i)
             pltpu.make_async_remote_copy(
                 src_ref=tc.at[c, k, pl.ds(0, 2)], dst_ref=tc.at[c, k, pl.ds(2 * d, 2)],
                 send_sem=ay_send.at[c], recv_sem=ay_recv.at[c], device_id=chip(-d, 0),
                 device_id_type=MESH).start()
 
+        @pl.when(c == LATE)
+        def _():
+            along_z(EARLY, NZ - 1)
+
     def gather_stage(c):
         local_wait(tc.at[c, k, pl.ds(2, PER - 2)], ay_recv.at[c])
+
         forward(c).start()
 
     def first_stage(c):
@@ -151,8 +169,9 @@
             pf[c, g] = p
             ps[c, :, g] = p.astype(BF)
 
-        @pl.loop(1, NX)
-        def _(r):
+        @pl.loop(0, NX - 1)
+        def _(i):
+            r = near(i)
             pltpu.make_async_remote_copy(
                 src_ref=ps.at[c, (x + r) % NX], dst_ref=pr.at[c, r - 1], send_sem=xr_send.at[c],
                 recv_sem=xr_recv.at[c], device_id=xpeer(r), device_id_type=MESH).start()
@@ -173,8 +192,9 @@
         hid[c, x, 1] = (slope * act).astype(BF)
         hid[c, x, 2] = (act * up).astype(BF)
 
-        @pl.loop(1, NX)
-        def _(r):
+        @pl.loop(0, NX - 1)
+        def _(i):
+            r = near(i)
             pltpu.make_async_remote_copy(
                 src_ref=hid.at[c, x], dst_ref=hid.at[c, x], send_sem=xa_send.at[c],
                 recv_sem=xa_recv.at[c], device_id=xpeer(r), device_id_type=MESH).start()
@@ -205,30 +225,42 @@
             def _():
                 yk[c, i] = both
 
-        @pl.loop(1, NY)
-        def _(d):
-            pltpu.make_async_remote_copy(
-                src_ref=rs.at[pl.ds(c * PER + 2 * d, 2)], dst_ref=yr.at[c, d - 1],
-                send_sem=sy_send.at[c], recv_sem=sy_recv.at[c], device_id=chip(d, 0),
-                device_id_type=MESH).start()
+        @pl.when(c < LAST)
+        def _():
+            @pl.loop(0, NY - 1)
+            def _(i):
+                d = near(i)
+                pltpu.make_async_remote_copy(
+                    src_ref=rs.at[pl.ds(c * PER + 2 * d, 2)], dst_ref=yr.at[c, d - 1],
+                    send_sem=sy_send.at[c], recv_sem=sy_recv.at[c], device_id=chip(d, 0),
+                    device_id_type=MESH).start()
+
+        @pl.when(c == LAST)
+        def _():
+            @pl.loop(1, PER)
+            def _(i):
+                pltpu.make_async_remote_copy(
+                    src_ref=rs.at[LAST * PER + i], dst_ref=lr.at[i - 1], send_sem=sy_send.at[LAST],
+                    recv_sem=sy_recv.at[LAST], device_id=chip(i // 2, zoff(2 * LAST + i % 2)),
+                    device_id_type=MESH).start()
 
     def settle_stage(c):
         local_wait(yr.at[c], sy_recv.at[c])
         two = yk[c] + jnp.sum(yr[c].astype(F32), axis=0)
         zs[pl.ds(2 * c, 2)] = two.astype(BF)
 
-        @pl.when(c == 0)
-        def _():
-            acc[...] = two[0]
-
-        @pl.loop(2 * c + jnp.where(c == 0, 1, 0), 2 * c + 2)
+        @pl.loop(2 * c, 2 * c + 2)
         def _(p):
             pltpu.make_async_remote_copy(
                 src_ref=zs.at[p], dst_ref=zr.at[p], send_sem=sz_send, recv_sem=sz_recv.at[c],
                 device_id=chip(0, zoff(p)), device_id_type=MESH).start()
 
+    def weight_stage(g):
+        h = jnp.concatenate([hid[c, :, g].reshape(fpad, CT) for c in range(CHUNKS)], axis=1)
+        wout[g] = jnp.dot(h, rows[g // 2], preferred_element_type=F32).astype(BF)
+
     stages = (spread_stage, gather_stage, first_stage, point_stage, second_stage,
-              scatter_stage, settle_stage)
+              scatter_stage, settle_stage, weight_stage)
 
     @pl.loop(0, len(ORDER))
     def _(i):
@@ -236,11 +268,6 @@
         c = lookup(1, i)
         for n, run in enumerate(stages):
             pl.when(stage == n)(lambda run=run: run(c))
-
-    @pl.loop(0, 3)
-    def _(g):
-        h = jnp.concatenate([hid[c, :, g].reshape(fpad, CT) for c in range(CHUNKS)], axis=1)
-        wout[g] = jnp.dot(h, rows[g // 2], preferred_element_type=F32).astype(BF)
 
     stores = [
         pltpu.make_async_copy(wout.at[0, pl.ds(0, ff)], dgu_hbm.at[0], o_sem.at[0]),
@@ -250,22 +277,28 @@
     for c in stores:
         c.start()
 
-    local_wait(zr.at[1], sz_recv.at[0])
-    acc[...] += zr[1].astype(F32)
-    for c in range(1, CHUNKS):
+    acc[...] = yk[LAST, 0]
+    for c in range(LAST):
         local_wait(zr.at[pl.ds(2 * c, 2)], sz_recv.at[c])
         acc[...] += zr[2 * c].astype(F32) + zr[2 * c + 1].astype(F32)
+    local_wait(lr, sy_recv.at[LAST])
+    acc[...] += jnp.sum(lr[...].astype(F32), axis=0)
 
     out_ref[...] = acc[0:8].astype(BF)
     dtok_ref[...] = acc[8:16].astype(BF)
 
-    local_wait(zr.at[pl.ds(0, NZ - 1)], az_send)
-    local_wait(zr.at[pl.ds(0, NZ - 1)], sz_send)
+    local_wait(lr, az_send)
+    local_wait(zr, sz_send)
+    local_wait(lr, sy_send.at[LAST])
 
     @pl.loop(0, CHUNKS)
     def _(c):
-        local_wait(yr.at[c], ay_send.at[c])
-        local_wait(yr.at[c], sy_send.at[c])
+        local_wait(yr.at[0], ay_send.at[c])
+
+        @pl.when(c < LAST)
+        def _():
+            local_wait(yr.at[0], sy_send.at[c])
+
         forward(c).wait_send()
         local_wait(pr.at[c], xr_send.at[c])
         local_wait(pr.at[c], xa_send.at[c])
@@ -329,9 +362,10 @@
             pltpu.VMEM((CHUNKS, 2, HALF, d), F32),
             pltpu.VMEM((CHIPS, ROWS, d), BF),
             pltpu.VMEM((CHUNKS, 2, ROWS, d), F32),
-            pltpu.VMEM((CHUNKS, NY - 1, 2, ROWS, d), BF),
-            pltpu.VMEM((NZ, ROWS, d), BF),
-            pltpu.VMEM((NZ, ROWS, d), BF),
+            pltpu.VMEM((CHUNKS - 1, NY - 1, 2, ROWS, d), BF),
+            pltpu.VMEM((NZ - 2, ROWS, d), BF),
+            pltpu.VMEM((NZ - 2, ROWS, d), BF),
+            pltpu.VMEM((PER - 1, ROWS, d), BF),
             pltpu.VMEM((ROWS, d), F32),
             dma((3,)), dma((3,)),
             dma, dma((CHUNKS,)), dma((CHUNKS,)), dma((CHUNKS,)), dma((CHUNKS,)), dma((CHUNKS,)),

time: 77.8 us -> 73.3 us (0.942); the launches traced: 76.8 us -> 73.2 us
  Pallas kernels: 76.2 us -> 72.5 us
    pallas_call x1, Pallas kernels: 73.2 us -> 69.6 us  [local(): pl.pallas_call(kernel, out_shape=(jax.ShapeDtypeStruct((rows, d), BF), ja...]
where the time goes in v3:
time: 73.3 us; the launch traced here: 73.2 us
  Pallas kernels  72.5 us (99%)
    pallas_call x1, Pallas kernels, local(): pl.pallas_call(kernel, out_shape=(jax.ShapeDtypeStruct((rows, d), BF), ja...  69.6 us
    pallas_call x1, Pallas kernels, local(): pl.pallas_call(deliver, out_shape=tuple((jax.ShapeDtypeStruct(r.shape, r....  2.95 us

profile of v3, /device:TPU:1, one launch (start us, length us, event | category | flops | bytes accessed | tf_op | source)
XLA Modules:
  0.0 73.2 jit_solution(3647663253689104324)
XLA Ops:
  0.6 69.6 %shard_map.75 = (bf16[8,1280]{1,0:T(8,128)(2,1)}, bf16[8,1280]{1,0:T(8,128)(2,1)}, bf16[2,432,1280]{2,1,0:T(8,128)(2,1)}, bf16[432,1280]{1,0:T(8,128)(2,1)}) custom-call(bf16[8,1280]{1,0:T(8,128)(2,1)} %tok_ref.1, bf16[8,1280]{1,0:T(8,128)(2,1)} %cot_ref.1, bf16[2,432,1280]{2,1,0:T(8,128)(2,1)} %wgu_hbm.1, bf16[432,1280]{1,0:T(8,128)(2,1)} %wd_hbm.1), custom_call_target="tpu_custom_call" | custom-call | tf_op jit(solution)/shard_map/pallas_call | solution.py:342
  70.2 2.9 %shard_map.76 = (bf16[8,1280]{1,0:T(8,128)(2,1)}, bf16[8,1280]{1,0:T(8,128)(2,1)}, bf16[2,432,1280]{2,1,0:T(8,128)(2,1)}, bf16[432,1280]{1,0:T(8,128)(2,1)}) custom-call(bf16[8,1280]{1,0:T(8,128)(2,1)} %get-tuple-element.8.refs_0_, bf16[8,1280]{1,0:T(8,128)(2,1)} %get-tuple-element.9.refs_1_, bf16[2,432,1280]{2,1,0:T(8,128)(2,1)} %get-tuple-element.10.refs_2_, ...), custom_call_target="tpu_custom_call" | custom-call | tf_op jit(solution)/shard_map/pallas_call | solution.py:379

commit v4 on v3

--- a/solution.py
+++ b/solution.py
@@ -15,8 +15,8 @@
 Z_ORDER = (7, 2, 6, 3, 5, 4, 0, 1)
 LAST = CHUNKS - 1
 ZTABLE = sum(d << (3 * i) for i, d in enumerate(Z_ORDER))
-ORDER = (0, 1, 10, 20, 2, 11, 21, 30, 3, 12, 22, 31, 40, 50, 13, 23, 32, 41, 60, 51, 33, 42, 61,
-         52, 43, 53, 62, 70, 71, 72)
+ORDER = (0, 1, 10, 20, 2, 11, 21, 12, 30, 3, 22, 31, 40, 50, 13, 23, 32, 41, 60, 51, 33, 42, 61,
+         52, 43, 70, 71, 53, 62, 72)
 EARLY, LATE = 4, 0
 WORD = 10
 
@@ -146,20 +146,24 @@
         def _():
             along_z(EARLY, NZ - 1)
 
+    def lay_rows(c, core):
+        @pl.loop(0, PER // 2)
+        def _(i):
+            two = tc[c, core, pl.ds(2 * i, 2)].astype(F32)
+            at = pl.ds(pl.multiple_of(c * CT + core * HALF + i * ROWS, ROWS), ROWS)
+            rows[0, at] = two[:, 0:8].reshape(ROWS, w.shape[2]).astype(BF)
+            rows[1, at] = two[:, 8:16].reshape(ROWS, w.shape[2]).astype(BF)
+
     def gather_stage(c):
         local_wait(tc.at[c, k, pl.ds(2, PER - 2)], ay_recv.at[c])
 
         forward(c).start()
+        lay_rows(c, k)
 
     def first_stage(c):
         local_wait(tc.at[c, 1 - k], fw_recv.at[c])
 
-        @pl.loop(0, PER)
-        def _(i):
-            two = tc[c, i // (PER // 2), pl.ds((i % (PER // 2)) * 2, 2)].astype(F32)
-            at = pl.ds(pl.multiple_of(c * CT + i * ROWS, ROWS), ROWS)
-            rows[0, at] = two[:, 0:8].reshape(ROWS, w.shape[2]).astype(BF)
-            rows[1, at] = two[:, 8:16].reshape(ROWS, w.shape[2]).astype(BF)
+        lay_rows(c, 1 - k)
 
         @pl.loop(0, 3)
         def _(g):
@@ -169,12 +173,13 @@
             pf[c, g] = p
             ps[c, :, g] = p.astype(BF)
 
-        @pl.loop(0, NX - 1)
-        def _(i):
-            r = near(i)
-            pltpu.make_async_remote_copy(
-                src_ref=ps.at[c, (x + r) % NX], dst_ref=pr.at[c, r - 1], send_sem=xr_send.at[c],
-                recv_sem=xr_recv.at[c], device_id=xpeer(r), device_id_type=MESH).start()
+            @pl.loop(0, NX - 1)
+            def _(i):
+                r = near(i)
+                pltpu.make_async_remote_copy(
+                    src_ref=ps.at[c, (x + r) % NX, g], dst_ref=pr.at[c, r - 1, g],
+                    send_sem=xr_send.at[c], recv_sem=xr_recv.at[c], device_id=xpeer(r),
+                    device_id_type=MESH).start()
 
     def point_stage(c):
         local_wait(pr.at[c], xr_recv.at[c])
@@ -255,9 +260,17 @@
                 src_ref=zs.at[p], dst_ref=zr.at[p], send_sem=sz_send, recv_sem=sz_recv.at[c],
                 device_id=chip(0, zoff(p)), device_id_type=MESH).start()
 
+    stores = [
+        pltpu.make_async_copy(wout.at[0, pl.ds(0, ff)], dgu_hbm.at[0], o_sem.at[0]),
+        pltpu.make_async_copy(wout.at[1, pl.ds(0, ff)], dgu_hbm.at[1], o_sem.at[1]),
+        pltpu.make_async_copy(wout.at[2, pl.ds(0, ff)], dd_hbm, o_sem.at[2]),
+    ]
+
     def weight_stage(g):
         h = jnp.concatenate([hid[c, :, g].reshape(fpad, CT) for c in range(CHUNKS)], axis=1)
         wout[g] = jnp.dot(h, rows[g // 2], preferred_element_type=F32).astype(BF)
+        for n, store in enumerate(stores):
+            pl.when(g == n)(store.start)
 
     stages = (spread_stage, gather_stage, first_stage, point_stage, second_stage,
               scatter_stage, settle_stage, weight_stage)
@@ -268,14 +281,6 @@
         c = lookup(1, i)
         for n, run in enumerate(stages):
             pl.when(stage == n)(lambda run=run: run(c))
-
-    stores = [
-        pltpu.make_async_copy(wout.at[0, pl.ds(0, ff)], dgu_hbm.at[0], o_sem.at[0]),
-        pltpu.make_async_copy(wout.at[1, pl.ds(0, ff)], dgu_hbm.at[1], o_sem.at[1]),
-        pltpu.make_async_copy(wout.at[2, pl.ds(0, ff)], dd_hbm, o_sem.at[2]),
-    ]
-    for c in stores:
-        c.start()
 
     acc[...] = yk[LAST, 0]
     for c in range(LAST):

time: 73.3 us -> 71.7 us (0.978)
  Pallas kernels: 72.5 us -> 70.9 us
    pallas_call x1, Pallas kernels: 69.6 us -> 68 us  [local(): pl.pallas_call(kernel, out_shape=(jax.ShapeDtypeStruct((rows, d), BF), ja...]
where the time goes in v4:
time: 71.7 us; the launch traced here: 71.5 us
  Pallas kernels  70.9 us (99%)
    pallas_call x1, Pallas kernels, local(): pl.pallas_call(kernel, out_shape=(jax.ShapeDtypeStruct((rows, d), BF), ja...  68 us
    pallas_call x1, Pallas kernels, local(): pl.pallas_call(deliver, out_shape=tuple((jax.ShapeDtypeStruct(r.shape, r....  2.95 us

profile of v4, /device:TPU:1, one launch (start us, length us, event | category | flops | bytes accessed | tf_op | source)
XLA Modules:
  0.0 71.5 jit_solution(9852379363083026776)
XLA Ops:
  0.6 68.0 %shard_map.75 = (bf16[8,1280]{1,0:T(8,128)(2,1)}, bf16[8,1280]{1,0:T(8,128)(2,1)}, bf16[2,432,1280]{2,1,0:T(8,128)(2,1)}, bf16[432,1280]{1,0:T(8,128)(2,1)}) custom-call(bf16[8,1280]{1,0:T(8,128)(2,1)} %tok_ref.1, bf16[8,1280]{1,0:T(8,128)(2,1)} %cot_ref.1, bf16[2,432,1280]{2,1,0:T(8,128)(2,1)} %wgu_hbm.1, bf16[432,1280]{1,0:T(8,128)(2,1)} %wd_hbm.1), custom_call_target="tpu_custom_call" | custom-call | tf_op jit(solution)/shard_map/pallas_call | solution.py:347
  68.6 2.9 %shard_map.76 = (bf16[8,1280]{1,0:T(8,128)(2,1)}, bf16[8,1280]{1,0:T(8,128)(2,1)}, bf16[2,432,1280]{2,1,0:T(8,128)(2,1)}, bf16[432,1280]{1,0:T(8,128)(2,1)}) custom-call(bf16[8,1280]{1,0:T(8,128)(2,1)} %get-tuple-element.8.refs_0_, bf16[8,1280]{1,0:T(8,128)(2,1)} %get-tuple-element.9.refs_1_, bf16[2,432,1280]{2,1,0:T(8,128)(2,1)} %get-tuple-element.10.refs_2_, ...), custom_call_target="tpu_custom_call" | custom-call | tf_op jit(solution)/shard_map/pallas_call | solution.py:384

commit v5 on v4

--- a/solution.py
+++ b/solution.py
@@ -181,6 +181,15 @@
                     send_sem=xr_send.at[c], recv_sem=xr_recv.at[c], device_id=xpeer(r),
                     device_id_type=MESH).start()
 
+    def share(c, which):
+        block = hid.at[c, x, which]
+
+        @pl.loop(0, NX - 1)
+        def _(i):
+            pltpu.make_async_remote_copy(
+                src_ref=block, dst_ref=block, send_sem=xa_send.at[c], recv_sem=xa_recv.at[c],
+                device_id=xpeer(near(i)), device_id_type=MESH).start()
+
     def point_stage(c):
         local_wait(pr.at[c], xr_recv.at[c])
 
@@ -193,16 +202,11 @@
         slope = total(2)
         sig = 1.0 / (1.0 + jnp.exp(-gate))
         act = gate * sig
+        hid[c, x, 2] = (act * up).astype(BF)
+        share(c, pl.ds(2, 1))
         hid[c, x, 0] = (slope * up * sig * (1.0 + gate * (1.0 - sig))).astype(BF)
         hid[c, x, 1] = (slope * act).astype(BF)
-        hid[c, x, 2] = (act * up).astype(BF)
-
-        @pl.loop(0, NX - 1)
-        def _(i):
-            r = near(i)
-            pltpu.make_async_remote_copy(
-                src_ref=hid.at[c, x], dst_ref=hid.at[c, x], send_sem=xa_send.at[c],
-                recv_sem=xa_recv.at[c], device_id=xpeer(r), device_id_type=MESH).start()
+        share(c, pl.ds(0, 2))
 
     def second_stage(c):
         local_wait(hid.at[c, pl.ds(0, NX - 1)], xa_recv.at[c])

time: 71.7 us -> 72.9 us (1.017)
  Pallas kernels: 70.9 us -> 72.1 us
    pallas_call x1, Pallas kernels: 68 us -> 69.1 us  [local(): pl.pallas_call(kernel, out_shape=(jax.ShapeDtypeStruct((rows, d), BF), ja...]
where the time goes in v5:
time: 72.9 us; the launch traced here: 72.7 us
  Pallas kernels  72.1 us (99%)
    pallas_call x1, Pallas kernels, local(): pl.pallas_call(kernel, out_shape=(jax.ShapeDtypeStruct((rows, d), BF), ja...  69.1 us
    pallas_call x1, Pallas kernels, local(): pl.pallas_call(deliver, out_shape=tuple((jax.ShapeDtypeStruct(r.shape, r....  2.95 us

profile of v5, /device:TPU:1, one launch (start us, length us, event | category | flops | bytes accessed | tf_op | source)
XLA Modules:
  0.0 72.7 jit_solution(14601140606401183762)
XLA Ops:
  0.6 69.1 %shard_map.75 = (bf16[8,1280]{1,0:T(8,128)(2,1)}, bf16[8,1280]{1,0:T(8,128)(2,1)}, bf16[2,432,1280]{2,1,0:T(8,128)(2,1)}, bf16[432,1280]{1,0:T(8,128)(2,1)}) custom-call(bf16[8,1280]{1,0:T(8,128)(2,1)} %tok_ref.1, bf16[8,1280]{1,0:T(8,128)(2,1)} %cot_ref.1, bf16[2,432,1280]{2,1,0:T(8,128)(2,1)} %wgu_hbm.1, bf16[432,1280]{1,0:T(8,128)(2,1)} %wd_hbm.1), custom_call_target="tpu_custom_call" | custom-call | tf_op jit(solution)/shard_map/pallas_call | solution.py:351
  69.8 2.9 %shard_map.76 = (bf16[8,1280]{1,0:T(8,128)(2,1)}, bf16[8,1280]{1,0:T(8,128)(2,1)}, bf16[2,432,1280]{2,1,0:T(8,128)(2,1)}, bf16[432,1280]{1,0:T(8,128)(2,1)}) custom-call(bf16[8,1280]{1,0:T(8,128)(2,1)} %get-tuple-element.8.refs_0_, bf16[8,1280]{1,0:T(8,128)(2,1)} %get-tuple-element.9.refs_1_, bf16[2,432,1280]{2,1,0:T(8,128)(2,1)} %get-tuple-element.10.refs_2_, ...), custom_call_target="tpu_custom_call" | custom-call | tf_op jit(solution)/shard_map/pallas_call | solution.py:388
